TPU v7x, 32 devices: a whole 2x2x4 slice. The times are simulated.
32 devices in a mesh: tok: 16 (over z, y, x), head: 2 (over core).
Axes of the slice: x: 2, y: 2, z: 4, core: 2. Of those that a mesh axis runs over, the one named last changes fastest.
Arguments:
- queries: bfloat16 [2, 12288, 1536], P(None, 'tok', 'head'), may hold values from -16 to 16
- key_rows: bfloat16 [2, 12288, 1536], P(None, 'tok', 'head'), may hold values from -8 to 8
- value_rows: bfloat16 [2, 12288, 1536], P(None, 'tok', 'head'), may hold values from -6 to 6
- step_rates: float32 [4, 2, 12288], P('head', None, 'tok'), may hold values from 0.01 to 1
- gate_init: float32 [4, 384, 384], P('head'), may hold values from -0.3125 to 0.3125
- up_init: float32 [4, 384, 384], P('head'), may hold values from -0.3125 to 0.3125
- down_init: float32 [4, 384, 384], P('head'), may hold values from -0.3125 to 0.3125
- out_weight: bfloat16 [1536, 1536], P('head'), may hold values from -0.15625 to 0.15625
Outputs:
- mixed_out: bfloat16 [2, 12288, 1536], P(None, 'tok', 'head')
All inputs are finite; a program needn't handle non-finite values.
Results may differ from a plain program's by a relative error of at most 0.009.
Values may be sent and summed in bfloat16 or wider, within the bound.
A program may use at most 128 MiB of HBM per device.

v0:
```python
import math

import jax
import jax.numpy as jnp
from jax import lax
from jax.sharding import PartitionSpec as P

DH = 384
WINDOW = 384


EPSILON = 1e-06


def shifted(x, axis, by):
    count = lax.axis_size(axis)
    return lax.ppermute(x, axis, [(i, (i + by) % count) for i in range(count)])


def silu_slope(values_in):
    sigmoid_at = jax.nn.sigmoid(values_in)
    return sigmoid_at * (1.0 + values_in * (1.0 - sigmoid_at))


def row_scale(matrix):
    return jnp.sqrt(jnp.mean(matrix * matrix, axis=-1, keepdims=True) + EPSILON)


def renormed(old_weight, gradient, rate_sum):
    updated = old_weight - gradient / rate_sum
    return updated * (row_scale(old_weight) / row_scale(updated))


def shards(queries, key_rows, value_rows, step_rates, gate_init, up_init, down_init, out_weight):
    blocks, local_rows, local_width = queries.shape
    heads_here = local_width // DH
    device_count = lax.axis_size("tok")
    device_at = lax.axis_index("tok")
    score_scale = 1.0 / math.sqrt(DH)
    tail_keys = key_rows[:, local_rows - WINDOW :, :]
    tail_values = value_rows[:, local_rows - WINDOW :, :]
    near_keys, near_values = shifted((tail_keys, tail_values), "tok", 1)
    is_first = device_at == 0
    near_keys = jnp.where(is_first, jnp.roll(near_keys, 1, axis=0), near_keys)
    near_values = jnp.where(is_first, jnp.roll(near_values, 1, axis=0), near_values)
    query_heads = queries.reshape(blocks, local_rows, heads_here, DH)
    key_heads = jnp.concatenate([near_keys, key_rows], axis=1).reshape(
        blocks, WINDOW + local_rows, heads_here, DH
    )
    value_heads = jnp.concatenate([near_values, value_rows], axis=1).reshape(
        blocks, WINDOW + local_rows, heads_here, DH
    )
    scores = (
        jnp.einsum("cqhd,ckhd->chqk", query_heads, key_heads, preferred_element_type=jnp.float32)
        * score_scale
    )
    offset = jnp.arange(WINDOW + local_rows)[None, :] - WINDOW - jnp.arange(local_rows)[:, None]
    block_first = jnp.arange(blocks) * (local_rows * device_count) + device_at * local_rows
    global_key = block_first[:, None] + jnp.arange(WINDOW + local_rows)[None, :] - WINDOW
    allowed = (offset <= 0) & (offset > -WINDOW)
    allowed = allowed[None, None] & (global_key >= 0)[:, None, None, :]
    scores = jnp.where(allowed, scores, -jnp.inf)
    row_max = jnp.max(scores, axis=-1, keepdims=True)
    expos = jnp.exp(scores - row_max)
    weights_bf = (expos / jnp.sum(expos, axis=-1, keepdims=True)).astype(jnp.bfloat16)
    attention = jnp.einsum(
        "chqk,ckhd->cqhd", weights_bf, value_heads, preferred_element_type=jnp.float32
    )
    cast_gate = gate_init.astype(jnp.bfloat16)
    cast_up = up_init.astype(jnp.bfloat16)
    cast_down = down_init.astype(jnp.bfloat16)
    gate_full, up_full, down_full = (gate_init, up_init, down_init)
    rate_totals = lax.psum(jnp.sum(step_rates, axis=2), "tok")
    head_blocks = []
    for block_at in range(blocks):
        rate_total = rate_totals[:, block_at]
        key_now = key_rows[block_at].reshape(local_rows, heads_here, DH)
        value_now = value_rows[block_at].reshape(local_rows, heads_here, DH)
        query_now = query_heads[block_at]
        errors = (
            jnp.transpose(step_rates[:, block_at, :])[:, :, None] * value_now.astype(jnp.float32)
        ).astype(jnp.bfloat16)
        pre_gate = jnp.einsum(
            "nhd,hfd->nhf", key_now, cast_gate, preferred_element_type=jnp.float32
        )
        pre_up = jnp.einsum("nhd,hfd->nhf", key_now, cast_up, preferred_element_type=jnp.float32)
        active = jax.nn.silu(pre_gate)
        hidden = (active * pre_up).astype(jnp.bfloat16)
        backed = jnp.einsum("nhd,hdf->nhf", errors, cast_down, preferred_element_type=jnp.float32)
        back_up = (-backed * active).astype(jnp.bfloat16)
        back_gate = (-backed * pre_up * silu_slope(pre_gate)).astype(jnp.bfloat16)
        grad_gate = jnp.einsum(
            "nhf,nhd->hfd", back_gate, key_now, preferred_element_type=jnp.float32
        )
        grad_up = jnp.einsum("nhf,nhd->hfd", back_up, key_now, preferred_element_type=jnp.float32)
        grad_down = -jnp.einsum("nhd,nhf->hdf", errors, hidden, preferred_element_type=jnp.float32)
        rate_shaped = rate_total[:, None, None]
        sum_gate, sum_up, sum_down = lax.psum((grad_gate, grad_up, grad_down), "tok")
        gate_full = renormed(gate_full, sum_gate, rate_shaped)
        up_full = renormed(up_full, sum_up, rate_shaped)
        down_full = renormed(down_full, sum_down, rate_shaped)
        cast_gate = gate_full.astype(jnp.bfloat16)
        cast_up = up_full.astype(jnp.bfloat16)
        cast_down = down_full.astype(jnp.bfloat16)
        query_gate = jnp.einsum(
            "nhd,hfd->nhf", query_now, cast_gate, preferred_element_type=jnp.float32
        )
        query_up = jnp.einsum(
            "nhd,hfd->nhf", query_now, cast_up, preferred_element_type=jnp.float32
        )
        query_hidden = (jax.nn.silu(query_gate) * query_up).astype(jnp.bfloat16)
        fast_out = jnp.einsum(
            "nhf,hdf->nhd", query_hidden, cast_down, preferred_element_type=jnp.float32
        )
        fast_out = fast_out / row_scale(fast_out)
        head_blocks.append(
            (fast_out + attention[block_at]).astype(jnp.bfloat16).reshape(local_rows, local_width)
        )
    joined = jnp.stack(head_blocks)
    partial_value = jnp.einsum(
        "cnw,wm->cnm", joined, out_weight, preferred_element_type=jnp.float32
    )
    mixed_out = lax.psum_scatter(partial_value, "head", scatter_dimension=2, tiled=True)
    return mixed_out.astype(jnp.bfloat16)


def solution(mesh):
    in_specs = (
        P(None, "tok", "head"),
        P(None, "tok", "head"),
        P(None, "tok", "head"),
        P("head", None, "tok"),
        P("head", None, None),
        P("head", None, None),
        P("head", None, None),
        P("head", None),
    )
    out_specs = P(None, "tok", "head")
    return jax.shard_map(shards, mesh=mesh, in_specs=in_specs, out_specs=out_specs, check_vma=False)
```

profile of v0, /device:TPU:0, one launch (start us, length us, event | category | flops | bytes accessed | tf_op | source)
XLA Modules:
  0.0 441.2 jit_solution(17129105009294027515)
XLA Ops:
  6.5 2.0 slice-done
  8.5 1.4 copy.155
  9.9 2.9 collective-permute-start
  12.8 4.3 copy.95
  17.1 2.6 slice.79
  19.7 1.5 collective-permute-start.1
  21.2 1.2 fusion.103
  22.4 0.9 copy-done.3
  23.3 2.5 slice_convert_fusion
  25.8 2.2 fusion.73
  28.0 2.2 fusion.75
  30.2 3.9 reshape.208
  34.1 0.6 fusion.106
  34.7 3.1 fusion.71
  37.8 1.8 fusion.55
  39.6 2.2 fusion.62
  41.8 2.6 convolution_negate_fusion.1
  44.4 0.0 all-reduce.7.cloned.1.call-update
  44.4 0.0 all-reduce.5.cloned.1.call-start
  44.5 1.8 fusion.8
  46.3 0.7 add_compare_fusion
  47.0 0.1 reduce_sum.144
  47.1 2.8 fusion.102
  49.9 69.8 %psum.50 = f32[2,2]{1,0:T(2,128)S(1)} all-reduce(f32[2,2]{1,0:T(2,128)S(1)} %reduce_sum.144), channel_id=1, replica_groups=mesh['tok'=16,'head'=2] {'tok'}, use_global_device_ids=true, to_apply=%region_2.3 | all-reduce | flops 4 | bytes 32 | tf_op jit(solution)/shard_map/psum | solution.py:73
  119.7 2.4 copy.154
  122.1 1.5 copy.156
  123.5 4.0 reshape.209
  127.5 0.6 copy.182
  128.1 0.2 slice_reduce_fusion
  128.3 2.0 broadcast_and_fusion
  130.3 1.4 fusion.105
  131.7 1.4 fusion.104
  133.0 1.4 maximum_select_fusion
  134.5 0.7 copy-done.2
  135.1 2.0 pad_maximum_fusion.1
  137.2 76.8 %all-reduce.7.cloned.1.call-done = (f32[2,384,384]{2,1,0:T(8,128)}, f32[2,384,384]{2,1,0:T(8,128)}, f32[2,384,384]{2,1,0:T(8,128)}) async-done(((f32[2,384,384]{2,1,0:T(8,128)}, f32[2,384,384]{2,1,0:T(8,128)}, f32[2,384,384]{2,1,0:T(8,128)}), (f32[2,384,384]{2,1,0:T(8,128)}, f32[2,384,384]{2,1,0:T(8,128)}, f32[2,384,384]{2,1,0:T(8,128)})) %all-reduce.7.cloned.1.call-update) | async-done | bytes 3538960 | tf_op jit(solution)/shard_map/psum | solution.py:98
  214.0 4.0 multiply_reduce_fusion.8
  218.1 0.8 fusion.88
  219.0 0.2 copy-done.5
  219.2 0.8 fusion.86
  220.0 0.8 copy-done.8
  220.8 1.5 fusion.83
  222.3 1.8 fusion.58
  224.2 2.1 fusion.64
  226.3 2.5 convolution_negate_fusion
  228.8 0.3 reduce-scatter.2.cloned.1.call-start
  229.1 13.0 %fusion.107 = (f32[2,2,768]{2,1,0:T(2,128)}, f32[2,2,768,1152]{2,3,1,0:T(8,128)}) fusion(pred[2,768,1152]{1,2,0:T(8,128)(4,1)} %broadcast_and_fusion, bf16[2,1152,2,384]{1,3,2,0:T(8,128)(2,1)} %bitcast.234, bf16[2,96,2,8,384]{4,3,2,1,0:T(8,128)(2,1)} %bitcast.236), kind=kOutput, calls=%fused_computation.168 | convolution fusion | flops 2732065792 | bytes 21835776 | tf_op jit(solution)/shard_map/sub | solution.py:64
  242.1 2.4 copy.108
  244.5 4.0 pad_maximum_fusion
  248.5 5.8 %copy.109 = bf16[2,1152,768]{1,2,0:T(8,128)(2,1)} copy(bf16[2,1152,768]{2,1,0:T(8,128)(2,1)} %pad_maximum_fusion) | data formatting | bytes 7077888 | tf_op jit(solution)/shard_map/concatenate | solution.py:50
  254.2 11.6 %fusion.51 = f32[2,768,2,384]{1,3,2,0:T(8,128)} fusion(bf16[2,1152,2,384]{1,3,2,0:T(8,128)(2,1)} %bitcast.235, f32[2,2,768,1152]{2,3,1,0:T(8,128)} %get-tuple-element.53, f32[2,2,768]{2,1,0:T(2,128)} %get-tuple-element.52), kind=kOutput, calls=%fused_computation.84 | convolution fusion | flops 2724986880 | bytes 22425600 | tf_op jit(solution)/shard_map/chqk,ckhd->cqhd/dot_general | solution.py:66
  265.9 2.2 fusion.87
  268.1 6.3 %fusion.35 = (f32[768,2]{0,1:T(2,128)}, f32[2,384,768]{2,1,0:T(8,128)}) fusion(f32[2,384,768]{2,1,0:T(8,128)} %fusion.87, bf16[768,2,384]{0,2,1:T(8,128)(2,1)} %bitcast.232, f32[2,384,384]{2,1,0:T(8,128)} %copy-done.5, f32[2,384]{1,0:T(2,128)S(1)} %get-tuple-element.60, f32[2,384,384]{2,1,0:T(8,128)} %copy-done.4, f32[2,384]{1,0:T(2,128)S(1)} %rsqrt_multiply_fusion.5), kind=kOutput, calls=%fused_computation.57 | convolution fusion | flops 911866368 | bytes 8269824 | tf_op jit(solution)/shard_map/nhf,hdf->nhd/dot_general | solution.py:112
  274.5 1.3 add_sqrt_fusion.1
  275.8 107.8 %all-reduce.5.cloned.1.call-done = (f32[2,384,384]{2,1,0:T(8,128)}, f32[2,384,384]{2,1,0:T(8,128)}, f32[2,384,384]{2,1,0:T(8,128)}) async-done(((f32[2,384,384]{2,1,0:T(8,128)}, f32[2,384,384]{2,1,0:T(8,128)}, f32[2,384,384]{2,1,0:T(8,128)}), (f32[2,384,384]{2,1,0:T(8,128)}, f32[2,384,384]{2,1,0:T(8,128)}, f32[2,384,384]{2,1,0:T(8,128)})) %all-reduce.5.cloned.1.call-update) | async-done | bytes 3538960 | tf_op jit(solution)/shard_map/psum | solution.py:98
  383.5 3.8 multiply_reduce_fusion.5
  387.4 2.3 fusion.66
  389.7 6.6 %fusion.21 = (f32[768,2]{0,1:T(2,128)S(1)}, f32[2,384,768]{2,1,0:T(8,128)}) fusion(f32[2,384,768]{2,1,0:T(8,128)} %fusion.66, bf16[768,2,384]{0,2,1:T(8,128)(2,1)} %bitcast.237, f32[2,384]{1,0:T(2,128)S(1)} %rsqrt_multiply_fusion, f32[2,384,384]{2,1,0:T(8,128)} %get-tuple-element.14, f32[2,384,384]{2,1,0:T(8,128)} %copy-done.5, ...), kind=kOutput, calls=%fused_computation.32 | convolution fusion | flops 913635840 | bytes 10635272 | tf_op jit(solution)/shard_map/nhf,hdf->nhd/dot_general | solution.py:112
  396.4 5.5 %fusion.15 = (bf16[768,2,384]{0,2,1:T(8,128)(2,1)S(1)}, bf16[768,2,384]{0,2,1:T(8,128)(2,1)}) fusion(f32[2,768,2,384]{1,3,2,0:T(8,128)} %fusion.51, f32[2,384,768]{2,1,0:T(8,128)} %get-tuple-element.55, f32[768,2]{0,1:T(2,128)} %add_sqrt_fusion.1, f32[768,2]{0,1:T(2,128)S(1)} %add_sqrt_fusion, f32[2,384,768]{2,1,0:T(8,128)} %get-tuple-element.57), kind=kLoop, calls=%fused_computation.24 | loop fusion | flops 3538944 | bytes 11808768 | tf_op jit(solution)/shard_map/convert_element_type | solution.py:117
  401.8 2.4 copy.129
  404.2 1.4 copy.128
  405.6 8.0 %fusion.16 = f32[2,768,1536]{2,1,0:T(8,128)} fusion(bf16[1,768,768]{2,1,0:T(8,128)(2,1)} %copy.129, bf16[1,768,768]{2,1,0:T(8,128)(2,1)} %copy.128, bf16[768,1536]{1,0:T(8,128)(2,1)S(1)} %copy-done), kind=kOutput, calls=%fused_computation.25 | convolution fusion | flops 3625058304 | bytes 14155776 | tf_op jit(solution)/shard_map/cnw,wm->cnm/dot_general | solution.py:120
  413.6 17.0 %reduce-scatter.2.cloned.1.call-done = f32[2,768,768]{2,1,0:T(8,128)} async-done(((f32[2,768,1536]{2,1,0:T(8,128)}), f32[2,768,768]{2,1,0:T(8,128)}) %reduce-scatter.2.cloned.1.call-update) | async-done | bytes 4718608 | tf_op jit(solution)/shard_map/reduce_scatter | solution.py:123
  430.7 4.0 convert_element_type.107
  (53 shorter events, 0.2 us)
Async XLA Ops:
  6.5 399.1 %copy-start = (bf16[768,1536]{1,0:T(8,128)(2,1)S(1)}, bf16[768,1536]{1,0:T(8,128)(2,1)}, u32[]{:S(2)}) copy-start(bf16[768,1536]{1,0:T(8,128)(2,1)} %param.15) | copy-start | bytes 7077892
  6.5 2.0 slice-start
  6.5 207.5 %all-reduce.7.cloned.1.call-start = ((), (), s32[]{:S(2)}) async-start(), calls=%async_computation.3 | async-start | bytes 7077888 | tf_op jit(solution)/shard_map/psum | solution.py:98
  9.9 120.4 %collective-permute-start = (bf16[2,384,768]{1,2,0:T(8,128)(2,1)}, bf16[2,384,768]{1,2,0:T(8,128)(2,1)}, u32[]{:S(2)}, u32[]{:S(2)}) collective-permute-start(bf16[2,384,768]{1,2,0:T(8,128)(2,1)} %copy.155), channel_id=1, source_target_pairs={{0,2},{2,4},{4,6},{6,8},{8,10},{10,12},{12,14},{14,16},{16,18},{18... | collective-permute-start | bytes 3538952 | tf_op jit(solution)/shard_map/ppermute | solution.py:17
  17.1 4.1 copy-start.1
  19.7 112.0 %collective-permute-start.1 = (bf16[2,384,768]{1,2,0:T(8,128)(2,1)}, bf16[2,384,768]{1,2,0:T(8,128)(2,1)}, u32[]{:S(2)}, u32[]{:S(2)}) collective-permute-start(bf16[2,384,768]{1,2,0:T(8,128)(2,1)} %slice.79), channel_id=1, source_target_pairs={{0,2},{2,4},{4,6},{6,8},{8,10},{10,12},{12,14},{14,16},{16,18},{18... | collective-permute-start | bytes 3538952 | tf_op jit(solution)/shard_map/ppermute | solution.py:17
  21.2 2.1 copy-start.3
  23.3 2.5 copy-start.9
  25.8 2.2 copy-start.10
  30.2 3.9 copy-start.17
  34.7 3.1 copy-start.14
  37.8 1.8 copy-start.13
  39.6 2.2 copy-start.7
  44.4 339.1 %all-reduce.5.cloned.1.call-start = ((), (), s32[]{:S(2)}) async-start(), calls=%async_computation.2 | async-start | bytes 7077888 | tf_op jit(solution)/shard_map/psum | solution.py:98
  123.5 4.0 copy-start.19
  123.5 4.8 %copy-start.12 = (pred[768,1152]{0,1:T(8,128)(4,1)S(1)}, pred[768,1152]{0,1:T(8,128)(4,1)}, u32[]{:S(2)}) copy-start(pred[768,1152]{0,1:T(8,128)(4,1)} %fusion.8) | copy-start | bytes 2654212
  123.5 4.8 %copy-start.20 = (pred[2,1152]{1,0:T(4,128)(4,1)S(1)}, pred[2,1152]{1,0:T(4,128)(4,1)}, u32[]{:S(2)}) copy-start(pred[2,1152]{1,0:T(4,128)(4,1)} %add_compare_fusion) | copy-start | bytes 6916
  133.0 2.1 copy-start.2
  214.0 4.1 copy-start.6
  218.0 1.1 copy-start.5
  218.1 1.9 copy-start.4
  219.2 1.7 copy-start.8
  219.2 1.7 copy-start.18
  228.8 201.8 %reduce-scatter.2.cloned.1.call-start = ((), (), s32[]{:S(2)}) async-start(), calls=%async_computation.1 | async-start | bytes 14155776 | tf_op jit(solution)/shard_map/reduce_scatter | solution.py:123
  254.2 11.6 %copy-start.11 = (bf16[1,768,768]{1,2,0:T(8,128)(2,1)S(1)}, bf16[1,768,768]{1,2,0:T(8,128)(2,1)}, u32[]{:S(2)}) copy-start(bf16[1,768,768]{1,2,0:T(8,128)(2,1)} %copy.154) | copy-start | bytes 3538948
  383.5 3.8 copy-start.15
  383.5 3.8 copy-start.16
Sparse Core Ops, SparseCore 0:
  44.6 169.4 all-reduce.6
  229.0 154.5 all-reduce.4
  413.8 16.8 reduce-scatter.1
where the time goes:
time: 442 us; the launch traced here: 441 us
  waiting for transfers between devices  202 us (46%)
  matrix products  73.8 us (17%)
  blocking collectives  69.8 us (16%)
  local copies, waits for them, and re-layouts  44.6 us (10%)
  other arithmetic  33.2 us (8%)
  between operations  13.3 us (3%)
  starting transfers between devices  4.74 us (1%)
    psum x2, waiting for transfers between devices, shards(): lax.psum((grad_gate, grad_up, grad_down), 'tok')  185 us
    psum x1, blocking collectives, shards(): rate_totals = lax.psum(jnp.sum(step_rates, axis=2), 'tok')  69.8 us
    reduce_scatter x1, waiting for transfers between devices, shards(): lax.psum_scatter(partial_value, 'head', scatter_dimension=2, tiled=True)  17 us
    sub x1, matrix products, shards(): expos = jnp.exp(scores - row_max)  13 us
    dot_general x2, matrix products, shards(): jnp.einsum('nhf,hdf->nhd', query_hidden, cast_down, preferred_element_typ...  13 us
    unnamed x48, local copies, waits for them, and re-layouts  12.7 us
    dot_general x1, matrix products, shards(): jnp.einsum('chqk,ckhd->cqhd', weights_bf, value_heads, preferred_element_...  11.6 us
  transfers between devices with their start and end apart: 5, of which 3 were waited for; matrix products, arithmetic and copies ran while one was open for 22% of the time, Pallas kernels for 0%

commit v1 on v0

v1 whole, which is shorter than its diff:
```python
import functools
import math

import jax
import jax.numpy as jnp
from jax import lax
from jax.experimental import pallas as pl
from jax.experimental.pallas import tpu as pltpu
from jax.sharding import PartitionSpec as P

DH = 384
WINDOW = 384
EPSILON = 1e-06
ROW_UNIT = 16
MESH = pl.DeviceIdType.MESH
NT = (((1,), (1,)), ((), ()))
NN = (((1,), (0,)), ((), ()))
TT = (((0,), (1,)), ((), ()))


def dot(a, b, dims):
    return lax.dot_general(a, b, dims, preferred_element_type=jnp.float32)


def sigmoid(x):
    return 0.5 * jnp.tanh(0.5 * x) + 0.5


def plan(bits, rows):
    orders = []
    for w in range(3):
        first = w % bits if bits else 0
        orders.append([first] + [j for j in range(bits) if j != first] if bits else [])
    sizes = [rows]
    for _ in range(bits):
        half = sizes[-1] // 2
        if sizes[-1] % 2 == 0 and half % ROW_UNIT == 0:
            sizes.append(half)
        else:
            break
    return orders, sizes


def kernel(
    bits, orders, sizes,
    q_ref, k_ref, v_ref, r_ref, g_ref, u_ref, d_ref, ow_ref,
    out_ref,
    halo_k, halo_v, att, wb, wf, grad, sb, rb, rate_sum, rate_in, ho, ho_peer, wo, wo_peer,
    rs_send, rs_recv, ag_send, ag_recv, halo_send, halo_recv, rate_send, rate_recv,
    ho_send, ho_recv, wo_send, wo_recv, local_sem,
):
    blocks, rows, width = q_ref.shape
    heads = width // DH
    tiles = rows // WINDOW
    count = lax.axis_size("tok")
    me = lax.axis_index("tok")
    core = lax.axis_index("head")
    peer = 1 - core
    nxt = lax.rem(me + 1, count)
    prv = lax.rem(me + count - 1, count)
    halvings = len(sizes) - 1
    cols = out_ref.shape[2]
    scale = 1.0 / math.sqrt(DH)

    bit = [lax.rem(lax.div(me, 2**j), 2) for j in range(bits)]
    partner = [me + (1 - 2 * bit[j]) * (2**j) for j in range(bits)]

    barrier = pltpu.get_barrier_semaphore()
    for j in range(bits):
        pl.semaphore_signal(barrier, inc=1, device_id={"tok": partner[j]}, device_id_type=MESH)
    pl.semaphore_signal(barrier, inc=1, device_id={"tok": nxt}, device_id_type=MESH)
    pl.semaphore_signal(barrier, inc=1, device_id={"tok": prv}, device_id_type=MESH)
    pl.semaphore_signal(barrier, inc=1, device_id={"head": peer}, device_id_type=MESH)
    pl.semaphore_wait(barrier, bits + 3)

    sent = []

    def remote(src, dst, ssem, rsem, device):
        return pltpu.make_async_remote_copy(
            src_ref=src, dst_ref=dst, send_sem=ssem, recv_sem=rsem,
            device_id=device, device_id_type=MESH,
        )

    def start(copy):
        copy.start()
        sent.append(copy)
        return copy

    offs = []
    for w in range(3):
        off = [0]
        for s in range(halvings):
            off.append(off[-1] + bit[orders[w][s]] * sizes[s + 1])
        offs.append([pl.multiple_of(o, ROW_UNIT) if i else 0 for i, o in enumerate(off)])
    region = [sum(sizes[1 : s + 1]) for s in range(halvings)]
    own = sizes[-1]
    for s in range(halvings, bits):
        region.append((region[-1] + (sizes[halvings] if s == halvings else own)) if region else 0)
    step_rows = [sizes[s + 1] if s < halvings else own for s in range(bits)]

    is_last = (me == count - 1).astype(jnp.int32)

    def halo(b):
        slot = lax.rem(b + is_last, blocks)
        for at, (src, dst) in enumerate(((k_ref, halo_k), (v_ref, halo_v))):
            start(remote(
                src.at[b, pl.ds(rows - WINDOW, WINDOW)], dst.at[slot],
                halo_send.at[at, b], halo_recv.at[at, slot], {"tok": nxt},
            ))

    def halo_wait(b):
        for at, (src, dst) in enumerate(((k_ref, halo_k), (v_ref, halo_v))):
            remote(
                src.at[b, pl.ds(rows - WINDOW, WINDOW)], dst.at[b],
                halo_send.at[at, b], halo_recv.at[at, b], {"tok": nxt},
            ).wait_recv()

    wo_local = pltpu.make_async_copy(
        ow_ref.at[:, pl.ds(pl.multiple_of(core * cols, 128), cols)], wo, local_sem
    )
    wo_local.start()
    wo_copy = start(remote(
        ow_ref.at[:, pl.ds(pl.multiple_of(peer * cols, 128), cols)], wo_peer,
        wo_send, wo_recv, {"head": peer},
    ))

    rate_sum[0] = jnp.zeros(rate_sum.shape[1:], jnp.float32)
    for h in range(heads):
        for b in range(blocks):
            total = jnp.sum(r_ref[h, b : b + 1, :], axis=1, keepdims=True)
            rate_sum[0, h * blocks + b : h * blocks + b + 1, :] = jnp.broadcast_to(total, (1, 128))

    def rate_copy(s):
        return remote(
            rate_sum.at[s], rate_in.at[s], rate_send.at[s], rate_recv.at[s], {"tok": partner[s]}
        )

    def rate_step(s):
        rate_copy(s).wait_recv()
        rate_sum[s + 1] = rate_sum[s] + rate_in[s]
        if s + 1 < bits:
            start(rate_copy(s + 1))

    def gradient(b, h):
        at = h * DH
        lanes = slice(at, at + DH)
        gate, up, down = wb[b, 3 * h], wb[b, 3 * h + 1], wb[b, 3 * h + 2]
        down_t = None
        for t in range(tiles):
            span = slice(t * WINDOW, (t + 1) * WINDOW)
            key = k_ref[b, span, lanes]
            value = v_ref[b, span, lanes]
            rate = r_ref[h, b : b + 1, span]
            h1 = dot(gate, key, NT)
            h3 = dot(up, key, NT)
            back = dot(down, value, TT) * rate
            sig = sigmoid(h1)
            active = h1 * sig
            hidden = (active * h3 * rate).astype(jnp.bfloat16)
            d3 = (back * active).astype(jnp.bfloat16)
            d1 = (back * h3 * (sig * (1.0 + h1 * (1.0 - sig)))).astype(jnp.bfloat16)
            t1, t3, t2 = dot(d1, key, NN), dot(d3, key, NN), dot(hidden, value, NN)
            if t == 0:
                grad[3 * h] = t1
                grad[3 * h + 1] = t3
                down_t = t2
            else:
                grad[3 * h] += t1
                grad[3 * h + 1] += t3
                down_t = down_t + t2
        grad[3 * h + 2] = down_t.T

    def rs_copy(b, h, w, s):
        i = 3 * h + w
        part = pl.ds(region[s], step_rows[s])
        return remote(
            sb.at[b, i, part], rb.at[b, i, part],
            rs_send.at[b, i, s], rs_recv.at[b, i, s], {"tok": partner[orders[w][s]]},
        )

    def rs_start(b, h, s):
        for w in range(3):
            i = 3 * h + w
            off = offs[w][min(s, halvings)]
            if s < halvings:
                off = off + (1 - bit[orders[w][s]]) * sizes[s + 1]
                off = pl.multiple_of(off, ROW_UNIT)
            piece = grad[i, pl.ds(off, step_rows[s]), :]
            sb[b, i, region[s] : region[s] + step_rows[s], :] = piece.astype(jnp.bfloat16)
            start(rs_copy(b, h, w, s))

    def rs_finish(b, h, s):
        for w in range(3):
            i = 3 * h + w
            rs_copy(b, h, w, s).wait_recv()
            got = rb[b, i, region[s] : region[s] + step_rows[s], :].astype(jnp.float32)
            keep = pl.ds(offs[w][min(s + 1, halvings)], step_rows[s])
            if s < halvings:
                grad[i, keep, :] = grad[i, keep, :] + got
            else:
                mine = sb[b, i, region[s] : region[s] + step_rows[s], :].astype(jnp.float32)
                grad[i, keep, :] = mine + got

    def row_mean(m):
        return jnp.mean(m * m, axis=1, keepdims=True) + EPSILON

    def update(b, h):
        row = h * blocks + b
        rate = rate_sum[bits, row : row + 1, 0:1]
        for w in range(3):
            i = 3 * h + w
            keep = pl.ds(offs[w][halvings], own)
            old = wf[i]
            new = old + grad[i, keep, :] / rate
            new = new * (jnp.sqrt(row_mean(old)) / jnp.sqrt(row_mean(new)))
            wf[i] = new
            wb[b + 1, i, keep, :] = new.astype(jnp.bfloat16)

    def ag_copy(b, h, w, s):
        i = 3 * h + w
        part = pl.ds(offs[w][s + 1], sizes[s + 1])
        return remote(
            wb.at[b + 1, i, part], wb.at[b + 1, i, part],
            ag_send.at[b, i, s], ag_recv.at[b, i, s], {"tok": partner[orders[w][s]]},
        )

    def ag_start(b, h, s):
        for w in range(3):
            start(ag_copy(b, h, w, s))

    def ag_finish(b, h, s):
        for w in range(3):
            ag_copy(b, h, w, s).wait_recv()

    row_at = lax.broadcasted_iota(jnp.int32, (WINDOW, WINDOW), 0)
    col_at = lax.broadcasted_iota(jnp.int32, (WINDOW, WINDOW), 1)

    def attend(b, h, t):
        lanes = slice(h * DH, (h + 1) * DH)
        span = slice(t * WINDOW, (t + 1) * WINDOW)
        query = q_ref[b, span, lanes]
        now = dot(query, k_ref[b, span, lanes], NT)
        if t == 0:
            before_k, before_v = halo_k[b, :, lanes], halo_v[b, :, lanes]
        else:
            earlier = slice((t - 1) * WINDOW, t * WINDOW)
            before_k, before_v = k_ref[b, earlier, lanes], v_ref[b, earlier, lanes]
        before = dot(query, before_k, NT)
        if t == 0 and b == 0:
            before = jnp.where(me == 0, -jnp.inf, before)
        here = col_at <= row_at
        scores = jnp.where(here, now, before) * scale
        expos = jnp.exp(scores - jnp.max(scores, axis=1, keepdims=True))
        probs = expos * (1.0 / jnp.sum(expos, axis=1, keepdims=True))
        near = jnp.where(here, probs, 0.0).astype(jnp.bfloat16)
        far = jnp.where(here, 0.0, probs).astype(jnp.bfloat16)
        att[b, span, lanes] = dot(near, v_ref[b, span, lanes], NN) + dot(far, before_v, NN)

    def ho_copy(b, h):
        part = (b, slice(None), pl.ds(h * DH, DH))
        return remote(
            ho.at[part], ho_peer.at[part], ho_send.at[b, h], ho_recv.at[b, h], {"head": peer}
        )

    def read_fast(b, h, t):
        lanes = slice(h * DH, (h + 1) * DH)
        span = slice(t * WINDOW, (t + 1) * WINDOW)
        query = q_ref[b, span, lanes]
        qg = dot(query, wb[b + 1, 3 * h], NT)
        qu = dot(query, wb[b + 1, 3 * h + 1], NT)
        hidden = (qg * sigmoid(qg) * qu).astype(jnp.bfloat16)
        fast = dot(hidden, wb[b + 1, 3 * h + 2], NT)
        fast = fast / jnp.sqrt(row_mean(fast))
        ho[b, span, lanes] = (fast + att[b, span, lanes]).astype(jnp.bfloat16)
        if t == tiles - 1:
            start(ho_copy(b, h))

    def project(b, t):
        span = slice(t * WINDOW, (t + 1) * WINDOW)
        total = dot(ho[b, span, :], wo[...], NN) + dot(ho_peer[b, span, :], wo_peer[...], NN)
        out_ref[b, span, :] = total.astype(jnp.bfloat16)

    halo(0)
    if bits:
        start(rate_copy(0))
    for h in range(heads):
        for w, init in enumerate((g_ref, u_ref, d_ref)):
            wb[0, 3 * h + w] = init[h].astype(jnp.bfloat16)
            wf[3 * h + w] = init[h, pl.ds(offs[w][halvings], own), :]

    part = functools.partial
    waiting = []
    for b in range(blocks):
        for t in range(1, tiles):
            for h in range(heads):
                waiting.append(part(attend, b, h, t))
    first_ready = len(waiting)
    del first_ready

    def halo_tiles(b):
        todo = [part(halo_wait, b)]
        todo += [part(attend, b, h, 0) for h in range(heads)]
        return todo

    def run(todo):
        if todo:
            todo.pop(0)()

    todo = list(waiting) + halo_tiles(0)
    for h in range(heads):
        gradient(0, h)
        rs_start(0, h, 0)
    for b in range(1, blocks):
        halo(b)
    for b in range(blocks):
        for s in range(bits):
            for h in range(heads):
                run(todo)
                rs_finish(b, h, s)
                if s + 1 < bits:
                    rs_start(b, h, s + 1)
            if b == 0:
                rate_step(s)
        for s in reversed(range(halvings)):
            for h in range(heads):
                if s == halvings - 1:
                    update(b, h)
                else:
                    ag_finish(b, h, s + 1)
                ag_start(b, h, s)
                run(todo)
        while todo:
            run(todo)
        for h in range(heads):
            if halvings:
                ag_finish(b, h, 0)
            if b + 1 < blocks:
                gradient(b + 1, h)
                rs_start(b + 1, h, 0)
        if b + 1 < blocks:
            todo = []
            for h in range(heads):
                todo += [part(read_fast, b, h, t) for t in range(tiles)]
            todo += halo_tiles(b + 1)
            if b == 0:
                todo.append(wo_local.wait)
                todo.append(wo_copy.wait_recv)
            todo += [ho_copy(b, h).wait_recv for h in range(heads)]
            todo += [part(project, b, t) for t in range(tiles)]
    last = blocks - 1
    if blocks == 1:
        wo_local.wait()
        wo_copy.wait_recv()
    for h in range(heads):
        for t in range(tiles):
            read_fast(last, h, t)
    for h in range(heads):
        ho_copy(last, h).wait_recv()
    for t in range(tiles):
        project(last, t)
    for copy in sent:
        copy.wait_send()


def shards(queries, key_rows, value_rows, step_rates, gate_init, up_init, down_init, out_weight):
    blocks, rows, width = queries.shape
    heads = width // DH
    count = lax.axis_size("tok")
    bits = count.bit_length() - 1
    cols = out_weight.shape[1] // lax.axis_size("head")
    orders, sizes = plan(bits, DH)
    halvings = len(sizes) - 1
    own = sizes[-1]
    staged = sum(sizes[1:]) + own * (bits - halvings)
    streams = 3 * heads
    bf16, f32 = jnp.bfloat16, jnp.float32
    dma = pltpu.SemaphoreType.DMA
    scratch = [
        pltpu.VMEM((blocks, WINDOW, width), bf16),
        pltpu.VMEM((blocks, WINDOW, width), bf16),
        pltpu.VMEM((blocks, rows, width), f32),
        pltpu.VMEM((blocks + 1, streams, DH, DH), bf16),
        pltpu.VMEM((streams, own, DH), f32),
        pltpu.VMEM((streams, DH, DH), f32),
        pltpu.VMEM((blocks, streams, staged, DH), bf16),
        pltpu.VMEM((blocks, streams, staged, DH), bf16),
        pltpu.VMEM((bits + 1, 8 * (-(-heads * blocks // 8)), 128), f32),
        pltpu.VMEM((bits, 8 * (-(-heads * blocks // 8)), 128), f32),
        pltpu.VMEM((blocks, rows, width), bf16),
        pltpu.VMEM((blocks, rows, width), bf16),
        pltpu.VMEM((out_weight.shape[0], cols), bf16),
        pltpu.VMEM((out_weight.shape[0], cols), bf16),
        dma((blocks, streams, bits)),
        dma((blocks, streams, bits)),
        dma((blocks, streams, halvings)),
        dma((blocks, streams, halvings)),
        dma((2, blocks)),
        dma((2, blocks)),
        dma((bits,)),
        dma((bits,)),
        dma((blocks, heads)),
        dma((blocks, heads)),
        dma,
        dma,
        dma,
    ]
    return pl.pallas_call(
        functools.partial(kernel, bits, orders, sizes),
        out_shape=jax.ShapeDtypeStruct((blocks, rows, cols), bf16),
        in_specs=[pl.BlockSpec(memory_space=pltpu.VMEM)] * 8,
        out_specs=pl.BlockSpec(memory_space=pltpu.VMEM),
        scratch_shapes=scratch,
        compiler_params=pltpu.CompilerParams(
            collective_id=0, has_side_effects=True, vmem_limit_bytes=60 * 1024 * 1024
        ),
        name="ttt_layer",
    )(queries, key_rows, value_rows, step_rates, gate_init, up_init, down_init, out_weight)


def solution(mesh):
    in_specs = (
        P(None, "tok", "head"),
        P(None, "tok", "head"),
        P(None, "tok", "head"),
        P("head", None, "tok"),
        P("head", None, None),
        P("head", None, None),
        P("head", None, None),
        P("head", None),
    )
    out_specs = P(None, "tok", "head")
    return jax.shard_map(shards, mesh=mesh, in_specs=in_specs, out_specs=out_specs, check_vma=False)
```

time: 442 us -> 158 us (0.36)
  waiting for transfers between devices: 202 us -> 0 us
  Pallas kernels: 0 us -> 153 us
  matrix products: 73.8 us -> 0 us
  blocking collectives: 69.8 us -> 0 us
  local copies, waits for them, and re-layouts: 44.6 us -> 3.22 us
  other arithmetic: 33.2 us -> 0 us
  between operations: 13.3 us -> 0.01 us
  starting transfers between devices: 4.74 us -> 0 us
    psum x2 -> x0, waiting for transfers between devices: 185 us -> none  [shards(): lax.psum((grad_gate, grad_up, grad_down), 'tok')]
    pallas_call x0 -> x1, Pallas kernels: none -> 153 us  [shards(): pl.pallas_call(functools.partial(kernel, bits, orders, sizes), out_shape=...]
    psum x1 -> x0, blocking collectives: 69.8 us -> none  [shards(): rate_totals = lax.psum(jnp.sum(step_rates, axis=2), 'tok')]
    dot_general x18 -> x0, matrix products: 60.8 us -> none  [the longest x2 13 us: shards(): jnp.einsum('nhf,hdf->nhd', query_hidden, cast_down, preferred_element_typ...]
    reduce_scatter x1 -> x0, waiting for transfers between devices: 17 us -> none  [shards(): lax.psum_scatter(partial_value, 'head', scatter_dimension=2, tiled=True)]
    sub x1 -> x0, matrix products: 13 us -> none  [shards(): expos = jnp.exp(scores - row_max)]
    slice x9 -> x0, local copies, waits for them, and re-layouts: 12.1 us -> none  [the longest x1 2.82 us: shards(): query_now = query_heads[block_at]]
    convert_element_type x3 -> x0, other arithmetic: 12 us -> none  [the longest x1 5.47 us: shards(): (fast_out + attention[block_at]).astype(jnp.bfloat16)]
  transfers between devices with their start and end apart: 5 -> 0, of which waited for: 3 -> 0; matrix products, arithmetic and copies ran while one was open for 22% -> 0% of each run, Pallas kernels for 0% -> 0%
where the time goes in v1:
time: 158 us; the launch traced here: 156 us
  Pallas kernels  153 us (97%)
  local copies, waits for them, and re-layouts  3.22 us (2%)
    pallas_call x1, Pallas kernels, shards(): pl.pallas_call(functools.partial(kernel, bits, orders, sizes), out_shape=...  153 us
    unnamed x1, local copies, waits for them, and re-layouts  3.22 us

profile of v1, /device:TPU:0, one launch (start us, length us, event | category | flops | bytes accessed | tf_op | source)
XLA Modules:
  0.0 156.5 jit_solution(6834142457153711065)
XLA Ops:
  0.0 153.3 %ttt_layer.1 = bf16[2,768,768]{2,1,0:T(8,128)(2,1)} custom-call(bf16[2,768,768]{2,1,0:T(8,128)(2,1)} %q_ref.1, bf16[2,768,768]{2,1,0:T(8,128)(2,1)} %k_ref.1, bf16[2,768,768]{2,1,0:T(8,128)(2,1)} %v_ref.1, f32[2,2,768]{2,1,0:T(2,128)} %r_ref.1, f32[2,384,384]{2,1,0:T(8,128)} %g_ref.1, f32[2,384,384]{2,1,0:T(8,128)} %u_ref.1, f32[2,384,384]{2,1,0:T(8,128)} %d_ref.1, ...), custom_call_target="tpu_custom_call" | custom-call | tf_op jit(solution)/shard_map/ttt_layer/pallas_call | solution.py:407
  153.3 3.2 %copy.10 = bf16[2,768,768]{2,1,0:T(8,128)(2,1)} copy(bf16[2,768,768]{2,1,0:T(8,128)(2,1)} %ttt_layer.1) | data formatting | bytes 4718592
